TPU v7x, 32 devices: a whole 2x2x4 slice. The times are simulated.
32 devices in a mesh: section: 4 (over y, x), tp: 2 (over core), dp: 4 (over z).
Axes of the slice: x: 2, y: 2, z: 4, core: 2. Of those that a mesh axis runs over, the one named last changes fastest.
Arguments:
- hidden_states: bfloat16 [672, 8192], P(None, 'dp'), may hold values from -120 to 120
- norm_gain: float32 [8192], P('dp'), may hold values from 0.5 to 1.5
- lm_head: bfloat16 [8192, 19008], P('dp', ('section', 'tp')), may hold values from -6 to 6
- target_ids: int32 [672], replicated, may hold values from 0 to 19007
Outputs:
- logprobs: bfloat16 [672, 19008], P(None, ('section', 'tp', 'dp'))
- target_logprob: float32 [672], P('dp')
All inputs are finite; a program needn't handle non-finite values.
Results may differ from a plain program's by a relative error of at most 0.0031.
Values may be sent and summed in bfloat16 or wider, within the bound.
A program may use at most 128 MiB of HBM per device.

v0:
```python
import jax
import jax.numpy as jnp
from jax import lax
from jax.sharding import PartitionSpec as P

D = 8192


epsilon = 1e-06


def local_terms(logits, targets, offset):
    columns = lax.broadcasted_iota(jnp.int32, logits.shape, 1) + offset
    return jnp.sum(jnp.where(columns == targets[:, None], logits, 0.0), axis=1)


def body(hidden_states, norm_gain, lm_head, target_ids):
    widened = hidden_states.astype(jnp.float32)
    squares = lax.psum(jnp.sum(widened * widened, axis=1), "dp")
    scale = lax.rsqrt(squares / D + epsilon)
    normed = (widened * scale[:, None] * norm_gain[None, :]).astype(jnp.bfloat16)
    row_count = normed.shape[0]
    block_width = lm_head.shape[1]
    dp_size = lax.axis_size("dp")
    own_rows = row_count // dp_size
    group_index = lax.axis_index("section") * lax.axis_size("tp") + lax.axis_index("tp")
    logits = lax.psum_scatter(
        jnp.dot(normed, lm_head, preferred_element_type=jnp.float32),
        "dp",
        scatter_dimension=0,
        tiled=True,
    )
    targets = lax.dynamic_slice_in_dim(target_ids, lax.axis_index("dp") * own_rows, own_rows, 0)
    picked = local_terms(logits, targets, group_index * block_width)
    row_top = lax.pmax(jnp.max(logits, axis=1), ("section", "tp"))
    row_total, picked = lax.psum(
        (jnp.sum(jnp.exp(logits - row_top[:, None]), axis=1), picked), ("section", "tp")
    )
    shifted = (logits - row_top[:, None] - jnp.log(row_total)[:, None]).astype(jnp.bfloat16)
    logprobs = lax.all_to_all(shifted, "dp", split_axis=1, concat_axis=0, tiled=True)
    target_logprob = picked - row_top - jnp.log(row_total)
    return (logprobs, target_logprob)


def solution(mesh):
    placed = (P(None, "dp"), P("dp"), P("dp", ("section", "tp")), P())
    return jax.shard_map(
        body,
        mesh=mesh,
        in_specs=placed,
        out_specs=(P(None, ("section", "tp", "dp")), P("dp")),
        check_vma=False,
    )
```

profile of v0, /device:TPU:0, one launch (start us, length us, event | category | flops | bytes accessed | tf_op | source)
XLA Modules:
  0.0 212.8 jit_solution(17433027478740349482)
XLA Ops:
  7.2 0.0 copy-start.1
  7.2 0.0 copy-start.2
  7.2 0.0 reduce-scatter.4.cloned.1.call-start
  7.2 2.5 %fusion = f32[672]{0:T(1024)S(1)} fusion(bf16[672,2048]{1,0:T(8,128)(2,1)} %param.4), kind=kLoop, calls=%fused_computation.2 | loop fusion | flops 4128096 | bytes 2755200 | tf_op jit(solution)/shard_map/reduce_sum | solution.py:19
  9.8 13.5 %psum.21 = f32[672]{0:T(1024)S(1)} all-reduce(f32[672]{0:T(1024)S(1)} %fusion), channel_id=1, replica_groups=mesh['section'=4,'tp'=2,'dp'=4] {'dp'}, use_global_device_ids=true, to_apply=%region_1.0 | all-reduce | flops 672 | bytes 5376 | tf_op jit(solution)/shard_map/psum | solution.py:19
  23.2 0.0 copy-done.1
  23.2 0.0 copy-done.2
  23.2 11.7 %fusion.3 = f32[672,2376]{1,0:T(8,128)} fusion(bf16[2048,2376]{0,1:T(8,128)(2,1)} %param.6, bf16[672,2048]{1,0:T(8,128)(2,1)S(1)} %copy-done.1, f32[2048]{0:T(1024)S(1)} %copy-done.2, f32[672]{0:T(1024)S(1)} %add_rsqrt_fusion), kind=kOutput, calls=%fused_computation.5 | convolution fusion | flops 6545473536 | bytes 18882176 | tf_op jit(solution)/shard_map/dot_general | solution.py:28
  35.0 0.0 reduce-scatter.4.cloned.1.call-update
  35.0 0.8 dynamic_slice.3
  35.8 112.5 %reduce-scatter.4.cloned.1.call-done = f32[168,2376]{1,0:T(8,128)} async-done(((f32[672,2376]{1,0:T(8,128)}), f32[168,2376]{1,0:T(8,128)}) %reduce-scatter.4.cloned.1.call-update) | async-done | bytes 1596688
  148.3 0.0 copy-start
  148.3 1.7 reduce_max.9
  150.0 13.6 %pmax.7 = f32[168]{0:T(256)S(1)} all-reduce(f32[168]{0:T(256)S(1)} %reduce_max.9), channel_id=1, replica_groups=mesh['section'=4,'tp'=2,'dp'=4] {'section','tp'}, use_global_device_ids=true, to_apply=%region_4.5 | all-reduce | flops 168 | bytes 1344 | tf_op jit(solution)/shard_map/pmax | solution.py:35
  163.6 2.0 select_reduce_fusion
  165.6 11.8 %all-reduce.1 = (f32[168]{0:T(256)S(1)}, f32[168]{0:T(256)S(1)}) all-reduce(f32[168]{0:T(256)S(1)} %get-tuple-element.3, f32[168]{0:T(256)S(1)} %get-tuple-element.2), channel_id=1, replica_groups=mesh['section'=4,'tp'=2,'dp'=4] {'section','tp'}, use_global_device_ids=true, to_apply=%region_6.7 | all-reduce | flops 336 | bytes 2688 | tf_op jit(solution)/shard_map/psum | solution.py:36
  177.4 0.6 subtract_subtract_fusion
  178.0 0.0 copy-done
  178.0 0.3 subtract_convert_fusion
  178.3 0.9 all_to_all.14
  179.2 0.1 copy.7
  179.3 25.7 %all_to_all.19 = bf16[168,4,594]{2,0,1:T(8,128)(2,1)S(1)} all-to-all(bf16[168,4,594]{2,0,1:T(8,128)(2,1)S(1)} %copy.7), channel_id=1, replica_groups=mesh['section'=4,'tp'=2,'dp'=4] {'dp'}, dimensions={1} | all-to-all | bytes 1596672 | tf_op jit(solution)/shard_map/all_to_all | solution.py:40
  205.0 0.9 copy.9
  (2 shorter events, 0.0 us)
Async XLA Ops:
  7.2 16.1 %copy-start.1 = (bf16[672,2048]{1,0:T(8,128)(2,1)S(1)}, bf16[672,2048]{1,0:T(8,128)(2,1)}, u32[]{:S(2)}) copy-start(bf16[672,2048]{1,0:T(8,128)(2,1)} %param.4) | copy-start | bytes 8257540
  7.2 16.1 %copy-start.2 = (f32[2048]{0:T(1024)S(1)}, f32[2048]{0:T(1024)}, u32[]{:S(2)}) copy-start(f32[2048]{0:T(1024)} %param.5) | copy-start | bytes 24580
  7.2 141.1 %reduce-scatter.4.cloned.1.call-start = ((), (), s32[]{:S(2)}) async-start(), calls=%async_computation.2 | async-start | bytes 8171520
  148.3 29.7 %copy-start = (f32[168,2376]{1,0:T(8,128)S(1)}, f32[168,2376]{1,0:T(8,128)}, u32[]{:S(2)}) copy-start(f32[168,2376]{1,0:T(8,128)} %reduce-scatter.4.cloned.1.call-done) | copy-start | bytes 4790020
Sparse Core Ops, SparseCore 0:
  35.1 113.1 reduce-scatter.3
where the time goes:
time: 213 us
  waiting for transfers between devices  113 us (53%)
  blocking collectives  64.6 us (30%)
  between operations  14.1 us (7%)
  matrix products  11.7 us (5%)
  other arithmetic  7.08 us (3%)
  local copies, waits for them, and re-layouts  2.71 us (1%)
    unnamed x2, waiting for transfers between devices  113 us
    all_to_all x1, blocking collectives, body(): lax.all_to_all(shifted, 'dp', split_axis=1, concat_axis=0, tiled=True)  25.7 us
    pmax x1, blocking collectives, body(): row_top = lax.pmax(jnp.max(logits, axis=1), ('section', 'tp'))  13.6 us
    psum x1, blocking collectives, body(): squares = lax.psum(jnp.sum(widened * widened, axis=1), 'dp')  13.5 us
    psum x1, blocking collectives, body(): lax.psum((jnp.sum(jnp.exp(logits - row_top[:, None]), axis=1), picked), (...  11.8 us
    dot_general x1, matrix products, body(): jnp.dot(normed, lm_head, preferred_element_type=jnp.float32)  11.7 us
  transfers between devices with their start and end apart: 1, of which 1 were waited for; matrix products, arithmetic and copies ran while one was open for 0% of the time, Pallas kernels for 0%

commit v1 on v0

v1 whole, which is shorter than its diff:
```python
import functools

import jax
import jax.numpy as jnp
from jax import lax
from jax.experimental import pallas as pl
from jax.experimental.pallas import tpu as pltpu
from jax.sharding import PartitionSpec as P

D = 8192

epsilon = 1e-06

MESH = pl.DeviceIdType.MESH
CHUNKS = 3
LANES = 128


def to_column(row):
    return jnp.broadcast_to(row, (LANES, row.shape[1])).T[:, :1]


def stack_rows(rows):
    place = lax.broadcasted_iota(jnp.int32, (8, rows[0].shape[1]), 0)
    result = jnp.zeros(place.shape, jnp.float32)
    for index, row in enumerate(rows):
        result = jnp.where(place == index, row, result)
    return result


def columns_to_rows(columns):
    place = lax.broadcasted_iota(jnp.int32, (columns[0].shape[0], LANES), 1)
    result = jnp.zeros(place.shape, jnp.float32)
    for index, column in enumerate(columns):
        result = jnp.where(place == index, column, result)
    return result.T[:8]


def merge(stats):
    tops, totals, picked = stats[:, 0:1], stats[:, 1:2], stats[:, 2:3]
    top = jnp.max(tops, axis=0)
    total = jnp.sum(totals * jnp.exp(tops - top[None]), axis=0)
    return top, total, jnp.sum(picked, axis=0)


def kernel(
    n, tp_size, plane, width, window, grain,
    x_hbm, w_hbm, gain_ref, target_ref,
    out_ref, target_out_ref,
    x_buf, w_buf, xg, part, send_buf, from_left, from_right, final, target_col,
    squares, all_squares, own_stats, plane_stats, own_merged, line_stats,
    load_sem, send_sem, left_sem, right_sem,
    sq_send, sq_recv, st_send, st_recv, ln_send, ln_recv,
):
    z = lax.axis_index("dp")
    me = lax.axis_index("section") * tp_size + lax.axis_index("tp")
    rc = xg.shape[1]

    load_x = pltpu.make_async_copy(x_hbm, x_buf, load_sem.at[0])
    load_w = pltpu.make_async_copy(w_hbm, w_buf, load_sem.at[1])
    load_x.start()
    load_w.start()

    def plane_peer(step):
        q = lax.rem(me + step, plane)
        return q, {"section": q // tp_size, "tp": lax.rem(q, tp_size)}

    def line_peer(step):
        q = lax.rem(z + step, n)
        return q, {"dp": q}

    barrier = pltpu.get_barrier_semaphore()

    def greet(peer, step, carry):
        pl.semaphore_signal(barrier, inc=1, device_id=peer(step)[1], device_id_type=MESH)
        return carry

    lax.fori_loop(1, plane, functools.partial(greet, plane_peer), 0)
    lax.fori_loop(1, n, functools.partial(greet, line_peer), 0)

    load_x.wait()
    gain = gain_ref[...]

    def prepare(r, carry):
        x = x_buf[pl.ds(pl.multiple_of(r * rc, 16), rc), :].astype(jnp.float32)
        xg[r] = (x * gain).astype(jnp.bfloat16)
        squares[r] = columns_to_rows([jnp.sum(x * x, axis=1, keepdims=True)])
        return carry

    lax.fori_loop(0, CHUNKS, prepare, 0)
    target_col[...] = jnp.broadcast_to(target_ref[...], (LANES, target_ref.shape[1])).T

    pl.semaphore_wait(barrier, plane - 1 + n - 1)

    def squares_copy(step, arriving):
        q, where = line_peer(step)
        return pltpu.make_async_remote_copy(
            src_ref=squares, dst_ref=all_squares.at[q if arriving else z],
            send_sem=sq_send.at[step], recv_sem=sq_recv.at[q if arriving else z],
            device_id=where, device_id_type=MESH,
        )

    def stats_copy(r, step, arriving):
        q, where = plane_peer(step)
        slot = q if arriving else me
        return pltpu.make_async_remote_copy(
            src_ref=own_stats.at[r], dst_ref=plane_stats.at[r, slot],
            send_sem=st_send.at[r, step], recv_sem=st_recv.at[r, slot],
            device_id=where, device_id_type=MESH,
        )

    def line_copy(r, step, arriving):
        q, where = line_peer(step)
        slot = q if arriving else z
        return pltpu.make_async_remote_copy(
            src_ref=own_merged.at[r], dst_ref=line_stats.at[r, slot],
            send_sem=ln_send.at[r, step], recv_sem=ln_recv.at[r, slot],
            device_id=where, device_id_type=MESH,
        )

    def each(first, last, action):
        def step_body(step, carry):
            action(step)
            return carry
        lax.fori_loop(first, last, step_body, 0)

    each(1, n, lambda step: squares_copy(step, False).start())
    all_squares[z] = squares[...]

    def right_copy(b, r):
        return pltpu.make_async_remote_copy(
            src_ref=send_buf.at[b, r], dst_ref=from_left.at[b, r],
            send_sem=send_sem.at[b, r], recv_sem=left_sem.at[b, r],
            device_id={"dp": lax.min(z + 1, n - 1)}, device_id_type=MESH,
        )

    def left_copy(b, r):
        return pltpu.make_async_remote_copy(
            src_ref=send_buf.at[b, r], dst_ref=from_right.at[b, r],
            send_sem=send_sem.at[b, r], recv_sem=right_sem.at[b, r],
            device_id={"dp": lax.max(z - 1, 0)}, device_id_type=MESH,
        )

    load_w.wait()

    def multiply(t, carry):
        r, i = t // n, lax.rem(t, n)
        b = jnp.where(z < n // 2, n - 1 - i, i)
        start = pl.multiple_of(width * b // grain * grain, grain)
        product = lax.dot_general(
            xg[r], w_buf[pl.ds(start, window), :],
            (((1,), (1,)), ((), ())), preferred_element_type=jnp.float32,
        )
        part[b, r] = product

        @pl.when((z == 0) & (b > 0))
        def _():
            send_buf[b, r] = product.astype(jnp.bfloat16)
            right_copy(b, r).start()

        @pl.when((z == n - 1) & (b < n - 1))
        def _():
            send_buf[b, r] = product.astype(jnp.bfloat16)
            left_copy(b, r).start()

        return carry

    lax.fori_loop(0, CHUNKS * n, multiply, 0)

    def forward(r, s):
        @pl.when((z >= 1) & (s >= z))
        def _():
            b = lax.min(n - 1 - s + z, n - 1)
            right_copy(b, r).wait_recv()
            send_buf[b, r] = (part[b, r] + from_left[b, r].astype(jnp.float32)).astype(jnp.bfloat16)
            right_copy(b, r).start()

        @pl.when((z <= n - 2) & (s >= n - 1 - z))
        def _():
            b = lax.max(s - (n - 1 - z), 0)
            left_copy(b, r).wait_recv()
            send_buf[b, r] = (part[b, r] + from_right[b, r].astype(jnp.float32)).astype(jnp.bfloat16)
            left_copy(b, r).start()

    padded = final.shape[2]

    def finish_sum(r):
        @pl.when(z >= 1)
        def _():
            right_copy(z, r).wait_recv()
            part[z, r] += from_left[z, r].astype(jnp.float32)

        @pl.when(z <= n - 2)
        def _():
            left_copy(z, r).wait_recv()
            part[z, r] += from_right[z, r].astype(jnp.float32)

        if r == 0:
            each(1, n, lambda step: squares_copy(step, True).wait_recv())
        total = jnp.sum(all_squares[:, r], axis=0)[0:1]
        scale = to_column(lax.rsqrt(total / D + epsilon))
        final[r, :, 0:window] = part[z, r] * scale
        moved = pltpu.roll(final[r], padded - (width * z - width * z // grain * grain), 1)
        final[r] = moved
        column = lax.broadcasted_iota(jnp.int32, moved.shape, 1)
        inside = column < width
        top = jnp.max(jnp.where(inside, moved, -jnp.inf), axis=1, keepdims=True)
        sum_exp = jnp.sum(jnp.where(inside, jnp.exp(moved - top), 0.0), axis=1, keepdims=True)
        wanted = target_col[r * rc:(r + 1) * rc, 0:1] - (me * n + z) * width
        hit = inside & (column == wanted)
        picked = jnp.sum(jnp.where(hit, moved, 0.0), axis=1, keepdims=True)
        stats = columns_to_rows([top, sum_exp, picked])
        own_stats[r] = stats
        plane_stats[r, me] = stats
        each(1, plane, lambda step: stats_copy(r, step, False).start())

    def merge_plane(r):
        each(1, plane, lambda step: stats_copy(r, step, True).wait_recv())
        merged = stack_rows(merge(plane_stats[r]))
        own_merged[r] = merged
        line_stats[r, z] = merged
        each(1, n, lambda step: line_copy(r, step, False).start())

    def emit(r):
        each(1, n, lambda step: line_copy(r, step, True).wait_recv())
        top, total, picked = merge(line_stats[r])
        norm = top + jnp.log(total)
        target_out_ref[r] = jnp.broadcast_to(picked - top - jnp.log(total), (8, rc))
        logprobs = final[r] - to_column(norm)
        out_ref[r * rc:(r + 1) * rc, :] = logprobs[:, :width].astype(jnp.bfloat16)

    final[...] = jnp.zeros(final.shape, jnp.float32)
    for r in range(CHUNKS):
        for s in range(1, n - 1):
            forward(r, s)
            if s == 1 and r >= 1:
                merge_plane(r - 1)
        if n == 2 and r >= 1:
            merge_plane(r - 1)
        if r >= 2:
            emit(r - 2)
        finish_sum(r)
    merge_plane(CHUNKS - 1)
    if CHUNKS >= 2:
        emit(CHUNKS - 2)
    emit(CHUNKS - 1)

    each(1, n, lambda step: squares_copy(step, False).wait_send())
    for r in range(CHUNKS):
        each(1, plane, lambda step: stats_copy(r, step, False).wait_send())
        each(1, n, lambda step: line_copy(r, step, False).wait_send())
        for b in range(n):
            @pl.when(b != z)
            def _():
                right_copy(b, r).wait_send()


def body(hidden_states, norm_gain, lm_head, target_ids):
    rows, depth = hidden_states.shape
    block = lm_head.shape[1]
    n, tp_size = lax.axis_size("dp"), lax.axis_size("tp")
    plane = lax.axis_size("section") * tp_size
    width = block // n
    grain = 16
    window = max(b * width % grain for b in range(n)) + width
    window = -(-window // 8) * 8
    assert (n - 1) * width // grain * grain + window <= block
    padded = -(-window // LANES) * LANES
    rc = rows // CHUNKS
    f32, bf16 = jnp.float32, jnp.bfloat16
    any_space = pl.BlockSpec(memory_space=pl.ANY)
    vmem = pl.BlockSpec(memory_space=pltpu.VMEM)
    dma = pltpu.SemaphoreType.DMA
    logprobs, target = pl.pallas_call(
        functools.partial(kernel, n, tp_size, plane, width, window, grain),
        out_shape=(
            jax.ShapeDtypeStruct((rows, width), bf16),
            jax.ShapeDtypeStruct((CHUNKS, 8, rc), f32),
        ),
        in_specs=[any_space, any_space, vmem, vmem],
        out_specs=(vmem, vmem),
        scratch_shapes=[
            pltpu.VMEM((rows, depth), bf16),
            pltpu.VMEM((block, depth), bf16),
            pltpu.VMEM((CHUNKS, rc, depth), bf16),
            pltpu.VMEM((n, CHUNKS, rc, window), f32),
            pltpu.VMEM((n, CHUNKS, rc, window), bf16),
            pltpu.VMEM((n, CHUNKS, rc, window), bf16),
            pltpu.VMEM((n, CHUNKS, rc, window), bf16),
            pltpu.VMEM((CHUNKS, rc, padded), f32),
            pltpu.VMEM((rows, LANES), jnp.int32),
            pltpu.VMEM((CHUNKS, 8, rc), f32),
            pltpu.VMEM((n, CHUNKS, 8, rc), f32),
            pltpu.VMEM((CHUNKS, 8, rc), f32),
            pltpu.VMEM((CHUNKS, plane, 8, rc), f32),
            pltpu.VMEM((CHUNKS, 8, rc), f32),
            pltpu.VMEM((CHUNKS, n, 8, rc), f32),
            dma((2,)),
            dma((n, CHUNKS)),
            dma((n, CHUNKS)),
            dma((n, CHUNKS)),
            dma((n,)),
            dma((n,)),
            dma((CHUNKS, plane)),
            dma((CHUNKS, plane)),
            dma((CHUNKS, n)),
            dma((CHUNKS, n)),
        ],
        compiler_params=pltpu.CompilerParams(
            collective_id=0, has_side_effects=True, vmem_limit_bytes=56 * 1024 * 1024
        ),
        cost_estimate=pl.CostEstimate(
            flops=2 * rows * depth * block,
            bytes_accessed=2 * (rows * depth + depth * block + rows * width),
            transcendentals=rows * width,
        ),
    )(hidden_states, lm_head.T, norm_gain[None, :], target_ids[None, :])
    own_rows = rows // n
    target = target[:, 0, :].reshape(rows)
    return logprobs, lax.dynamic_slice_in_dim(target, lax.axis_index("dp") * own_rows, own_rows, 0)


def solution(mesh):
    placed = (P(None, "dp"), P("dp"), P("dp", ("section", "tp")), P())
    return jax.shard_map(
        body,
        mesh=mesh,
        in_specs=placed,
        out_specs=(P(None, ("section", "tp", "dp")), P("dp")),
        check_vma=False,
    )
```

time: 213 us -> 84.6 us (0.40)
  waiting for transfers between devices: 113 us -> 0 us
  Pallas kernels: 0 us -> 78.8 us
  blocking collectives: 64.6 us -> 0 us
  between operations: 14.1 us -> 0.64 us
  matrix products: 11.7 us -> 0 us
  other arithmetic: 7.08 us -> 0 us
  local copies, waits for them, and re-layouts: 2.71 us -> 4.88 us
    unnamed x2 -> x0, waiting for transfers between devices: 113 us -> none
    pallas_call x0 -> x1, Pallas kernels: none -> 78.8 us  [body(): pl.pallas_call(functools.partial(kernel, n, tp_size, plane, width, window...]
    all_to_all x1 -> x0, blocking collectives: 25.7 us -> none  [body(): lax.all_to_all(shifted, 'dp', split_axis=1, concat_axis=0, tiled=True)]
    psum x2 -> x0, blocking collectives: 25.3 us -> none  [the longest x1 13.5 us: body(): squares = lax.psum(jnp.sum(widened * widened, axis=1), 'dp')]
    pmax x1 -> x0, blocking collectives: 13.6 us -> none  [body(): row_top = lax.pmax(jnp.max(logits, axis=1), ('section', 'tp'))]
    dot_general x1 -> x0, matrix products: 11.7 us -> none  [body(): jnp.dot(normed, lm_head, preferred_element_type=jnp.float32)]
    reduce_sum x2 -> x0, other arithmetic: 4.52 us -> none  [the longest x1 2.53 us: body(): squares = lax.psum(jnp.sum(widened * widened, axis=1), 'dp')]
  transfers between devices with their start and end apart: 1 -> 0, of which waited for: 1 -> 0; matrix products, arithmetic and copies ran while one was open for 0% -> 0% of each run, Pallas kernels for 0% -> 0%
where the time goes in v1:
time: 84.6 us; the launch traced here: 84.3 us
  Pallas kernels  78.8 us (93%)
  local copies, waits for them, and re-layouts  4.88 us (6%)
    pallas_call x1, Pallas kernels, body(): pl.pallas_call(functools.partial(kernel, n, tp_size, plane, width, window...  78.8 us
    unnamed x1, local copies, waits for them, and re-layouts  2.14 us

profile of v1, /device:TPU:0, one launch (start us, length us, event | category | flops | bytes accessed | tf_op | source)
XLA Modules:
  0.0 84.3 jit_solution(13718091178815623925)
XLA Ops:
  0.6 1.3 %broadcast_in_dim.7.target_ref = s32[1,672]{1,0:T(1,128)} reshape(s32[672]{0:T(1024)} %param.7) | data formatting | bytes 5376 | tf_op jit(solution)/shard_map/broadcast_in_dim | solution.py:317
  1.9 78.8 %shard_map.59 = (bf16[672,594]{1,0:T(8,128)(2,1)}, f32[3,8,224]{2,1,0:T(8,128)}) custom-call(bf16[672,2048]{1,0:T(8,128)(2,1)} %x_hbm.1, bf16[2376,2048]{1,0:T(8,128)(2,1)} %bitcast.2, f32[1,2048]{1,0:T(1,128)} %bitcast.3, s32[1,672]{1,0:T(1,128)} %broadcast_in_dim.7.target_ref), custom_call_target="tpu_custom_call" | custom-call | flops 6539968512 | bytes 13282944 | tf_op jit(solution)/shard_map/pallas_call | solution.py:274
  80.7 0.8 slice_reduce_fusion
  81.4 0.1 reshape_squeeze.3
  81.5 0.6 dynamic_slice.3
  82.2 2.1 %copy.7 = bf16[672,594]{1,0:T(8,128)(2,1)} copy(bf16[672,594]{1,0:T(8,128)(2,1)} %get-tuple-element.8) | data formatting | bytes 1596672
